TPU v7x, 32 devices: a whole 2x2x4 slice. The times are simulated.
32 devices in a mesh: tok: 4 (over z), head: 4 (over y, x), grp: 2 (over core).
Axes of the slice: x: 2, y: 2, z: 4, core: 2. Of those that a mesh axis runs over, the one named last changes fastest.
Arguments:
- tokens: bfloat16 [2048, 4096], P('tok', ('head', 'grp')), may hold values from -6 to 6
- norm_gain: bfloat16 [4096], P(('head', 'grp')), may hold values from 1.2 to 9, as said below
- query_key_value_weight: bfloat16 [4096, 6144], P(None, ('head', 'grp')), may hold values from -0.09375 to 0.09375
- out_weight: bfloat16 [4096, 4096], P(('head', 'grp')), may hold values from -0.09375 to 0.09375
- doc_ids: int32 [2048], P('tok'), may hold values from 0 to 3, never falling along the last dimension, each value on 1 to 1024 neighbouring positions
Outputs:
- attended: bfloat16 [2048, 4096], P('tok', ('head', 'grp'))
Inputs may be any that keep to these rules, and one draw needn't show every extreme that they name: `norm_gain`: norm gains are positive. `doc_ids`: non-decreasing along the window; each document has 1 to 1024 tokens and one has exactly 1024.
All inputs are finite; a program needn't handle non-finite values.
Results may differ from a plain program's by a relative error of at most 0.019.
The roundings to bfloat16 on the way count: a program that leaves them out, or rounds other values in their place, can miss the bound.
Values may be sent and summed in bfloat16 or wider, within the bound.
A program may use at most 128 MiB of HBM per device.

v0:
```python
import jax
import jax.numpy as jnp
from jax import lax
from jax.sharding import PartitionSpec as P

QUERY_HEADS = 32
KEY_VALUE_HEADS = 8
HEAD_SIZE = 128


epsilon = 1e-05
theta = 500000.0
floor_score = -1e30


def for_sending(array):

    def short(part):
        return part.astype(jnp.bfloat16) if part.dtype == jnp.float32 else part

    return jax.tree.map(short, array)


def passed_along(block, axis, distance):
    devices = range(lax.axis_size(axis))
    route = [((i - distance) % len(devices), i) for i in devices]
    return lax.ppermute(block, axis, route)


def rotate(vectors, positions):
    half = vectors.shape[-1] // 2
    inverse = 1.0 / theta ** (jnp.arange(half, dtype=jnp.float32) * (2.0 / vectors.shape[-1]))
    angles = positions.astype(jnp.float32)[:, None] * inverse[None, :]
    cosine = jnp.cos(angles)[:, None, :]
    sine = jnp.sin(angles)[:, None, :]
    first = vectors[..., :half]
    second = vectors[..., half:]
    return jnp.concatenate(
        [first * cosine - second * sine, second * cosine + first * sine], axis=-1
    )


def make_set(query_rows, positions, docs, head_group):
    length = query_rows.shape[0]
    flat = query_rows.reshape(length * head_group, query_rows.shape[1] // head_group)
    return (
        flat,
        jnp.repeat(positions, head_group),
        jnp.repeat(docs, head_group),
        docs[0],
        positions[length - 1],
    )


def empty_state(query_set):
    rows_all = query_set[0].shape[0]
    return (
        jnp.full((rows_all,), floor_score, jnp.float32),
        jnp.zeros((rows_all,), jnp.float32),
        jnp.zeros((rows_all, query_set[0].shape[1]), jnp.float32),
    )


def finish(state, head_group):
    highest, totals, accum = state
    normal = (accum / totals[:, None]).astype(jnp.bfloat16)
    return normal.reshape(normal.shape[0] // head_group, head_group * normal.shape[1])


def update(state, query_set, block_pairs, block_docs, block_positions):
    flat, query_positions, query_docs = (query_set[0], query_set[1], query_set[2])
    highest, totals, accum = state
    width = flat.shape[1]
    scores = lax.dot_general(
        flat, block_pairs[:, :width], (((1,), (1,)), ((), ())), preferred_element_type=jnp.float32
    ) * width ** (-0.5)
    mask = (block_positions[None, :] <= query_positions[:, None]) & (
        block_docs[None, :] == query_docs[:, None]
    )
    new_high = jnp.maximum(highest, jnp.max(jnp.where(mask, scores, floor_score), axis=1))
    weights = jnp.where(mask, jnp.exp(scores - new_high[:, None]), 0.0)
    fade = jnp.exp(highest - new_high)
    totals = totals * fade + jnp.sum(weights, axis=1)
    accum = accum * fade[:, None] + jnp.dot(
        weights.astype(jnp.bfloat16), block_pairs[:, width:], preferred_element_type=jnp.float32
    )
    return (new_high, totals, accum)


def fold_piece(state, query_set, pairs, docs, start):
    length = pairs.shape[0]
    width = 512

    def step(index, carried):
        offset = index * width
        first_key = start + offset
        block_positions = first_key + jnp.arange(width, dtype=jnp.int32)
        needed = (first_key <= query_set[4]) & (docs[width - 1] >= query_set[3])
        return lax.cond(
            needed,
            lambda held: update(held, query_set, pairs, docs, block_positions),
            lambda held: held,
            carried,
        )

    return lax.fori_loop(0, length // width, step, state)


def body(tokens, norm_gain, query_key_value_weight, out_weight, doc_ids):
    length = tokens.shape[0]
    head_group = QUERY_HEADS // KEY_VALUE_HEADS
    whole, gain = (
        lax.all_gather(tokens, ("head", "grp"), axis=1, tiled=True),
        lax.all_gather(norm_gain, ("head", "grp"), axis=0, tiled=True),
    )
    floats = whole.astype(jnp.float32)
    normed_input = (
        floats
        * lax.rsqrt(jnp.mean(floats * floats, axis=1, keepdims=True) + epsilon)
        * gain.astype(jnp.float32)
    ).astype(jnp.bfloat16)
    mixed_output = jnp.dot(normed_input, query_key_value_weight, preferred_element_type=jnp.float32)
    shard = lax.axis_index("tok")
    axis_size = lax.axis_size("tok")
    positions = shard * length + jnp.arange(length, dtype=jnp.int32)
    query_rows = (
        rotate(
            mixed_output[:, : head_group * HEAD_SIZE].reshape(length, head_group, HEAD_SIZE),
            positions,
        )
        .astype(jnp.bfloat16)
        .reshape(length, head_group * HEAD_SIZE)
    )
    keys = rotate(
        mixed_output[:, head_group * HEAD_SIZE : (head_group + 1) * HEAD_SIZE].reshape(
            length, 1, HEAD_SIZE
        ),
        positions,
    ).reshape(length, HEAD_SIZE)
    key_value = jnp.concatenate(
        [keys, mixed_output[:, (head_group + 1) * HEAD_SIZE :]], axis=1
    ).astype(jnp.bfloat16)
    query_sets = (make_set(query_rows, positions, doc_ids, head_group),)
    initial = tuple((empty_state(query_set) for query_set in query_sets))

    def fold_all(states, pieces, start):
        return tuple(
            (
                fold_piece(state, query_set, pieces[0], pieces[1], start)
                for state, query_set in zip(states, query_sets)
            )
        )

    reach = axis_size // 2
    first_states = fold_all(initial, (key_value, doc_ids), shard * length)

    def advance(step_index, carried):
        travelling, held = carried
        moved = jax.tree.map(
            lambda part, own: part.astype(own.dtype),
            passed_along(for_sending(travelling), "tok", 1),
            travelling,
        )
        anchor = jnp.mod(shard - step_index, axis_size)
        return (moved, fold_all(held, moved, anchor * length))

    states = lax.fori_loop(1, reach + 1, advance, ((key_value, doc_ids), first_states))[1]
    heads = finish(states[0], head_group)
    partial_products = jnp.dot(heads, out_weight, preferred_element_type=jnp.float32)
    return lax.psum_scatter(
        partial_products.astype(jnp.bfloat16), ("head", "grp"), scatter_dimension=1, tiled=True
    )


def solution(mesh):
    return jax.shard_map(
        body,
        mesh=mesh,
        in_specs=(
            P("tok", ("head", "grp")),
            P(("head", "grp")),
            P(None, ("head", "grp")),
            P(("head", "grp"), None),
            P("tok"),
        ),
        out_specs=P("tok", ("head", "grp")),
        check_vma=False,
    )
```

profile of v0, /device:TPU:16, one launch (start us, length us, event | category | flops | bytes accessed | tf_op | source)
XLA Modules:
  0.0 165.5 jit_solution(17726012028081998380)
XLA Ops:
  8.0 8.9 %all-gather = bf16[8,1,512]{2,1,0:T(2,128)(2,1)S(1)} all-gather(bf16[1,1,512]{2,1,0:T(2,128)(2,1)S(1)} %reshape.147), channel_id=1, replica_groups=mesh['tok'=4,'head'=4,'grp'=2] {'head','grp'}, dimensions={0}, use_global_device_ids=true | all-gather | bytes 9216 | tf_op jit(solution)/shard_map/all_gather | solution.py:114
  18.7 1.2 copy.26
  19.9 1.3 fusion.50
  22.7 1.8 %multiply_cosine_fusion = (f32[512,64]{1,0:T(8,128)S(1)}, f32[512,64]{1,0:T(8,128)}) fusion(f32[64]{0:T(128)S(1)} %negate_power_fusion, f32[512]{0:T(512)S(1)} %get-tuple-element.592), kind=kLoop, calls=%fused_computation.57 | loop fusion | flops 32768 | bytes 264448 | tf_op jit(solution)/shard_map/cos | solution.py:34
  24.4 23.3 %all-gather.3.cloned.1.call-done = bf16[512,4096]{1,0:T(8,128)(2,1)} async-done(((bf16[512,512]{1,0:T(8,128)(2,1)}), bf16[512,4096]{1,0:T(8,128)(2,1)}) %all-gather.3.cloned.1.call-update) | async-done | bytes 4194320 | tf_op jit(solution)/shard_map/all_gather | solution.py:113
  47.8 3.2 %fusion.34 = f32[512]{0:T(512)S(1)} fusion(bf16[512,4096]{1,0:T(8,128)(2,1)} %all-gather.3.cloned.1.call-done), kind=kLoop, calls=%fused_computation.45 | loop fusion | flops 6290944 | bytes 4196352 | tf_op jit(solution)/shard_map/reduce_sum | solution.py:119
  51.2 5.6 %fusion.37 = f32[512,768]{1,0:T(8,128)S(1)} fusion(bf16[4096,768]{1,0:T(8,128)(2,1)} %param.13, bf16[512,4096]{1,0:T(8,128)(2,1)S(1)} %copy-done, f32[4096]{0:T(1024)S(1)} %bitcast.20, f32[512]{0:T(512)S(1)} %add_rsqrt_fusion), kind=kOutput, calls=%fused_computation.49 | convolution fusion | flops 3229614080 | bytes 12077056 | tf_op jit(solution)/shard_map/dot_general | solution.py:122
  59.2 1.2 fusion.46
  61.5 1.8 %subtract_convert_fusion = (bf16[512,4,64]{2,1,0:T(4,128)(2,1)S(1)}, bf16[512,4,64]{2,1,0:T(4,128)(2,1)S(1)}) fusion(f32[512,4,128]{2,1,0:T(4,128)S(1)} %reshape.145, f32[512,64]{1,0:T(8,128)} %get-tuple-element.588, f32[512,64]{1,0:T(8,128)S(1)} %get-tuple-element.587), kind=kLoop, calls=%fused_computation.54 | loop fusion | flops 1048576 | bytes 1835008 | tf_op jit(solution)/shard_map/convert.3
  63.6 5.6 %conditional.2 = ((f32[2048]{0:T(1024)S(1)}, f32[2048]{0:T(1024)S(1)}, f32[2048,128]{1,0:T(8,128)S(1)})) conditional(s32[]{:T(128)} %convert_element_type.51, (f32[2048]{0:T(1024)S(1)}, f32[2048]{0:T(1024)S(1)}, f32[2048,128]{1,0:T(8,128)S(1)}) %tuple.47, (s32[512]{0:T(512)S(1)}, s32[512]{0:T(512)S(1)}, s32[512]{0:T(512)S(1)}, s32[512]{0:T(512)S(1)}, ...), branch_computations={%region_1.2_spmd, %region_2.5_spmd} | conditional | flops 558370816 | bytes 16236576 | solution.py:99
  64.4 1.1 select_reduce_fusion
  65.5 1.6 fusion.5
  67.1 1.8 %convolution_add_fusion = f32[2048,128]{1,0:T(8,128)S(1)} fusion(f32[2048,512]{0,1:T(8,128)S(1)} %get-tuple-element.580, f32[2048]{0:T(1024)S(1)} %max.4, s32[2048]{0:T(1024)S(1)} %eq.31, s32[2048]{0:T(1024)S(1)} %le.36, s32[512]{0:T(512)S(1)} %get-tuple-element.550, s32[512]{0:T(512)S(1)} %get-tuple-element.549, f32[2048,128]{1,0:T(8,128)S(1)} %get-tuple-element.457, ...), kind=kOutput, calls=%fused_computation.5 | convolution fusion | flops 276299776 | bytes 6459392 | tf_op jit(solution)/shard_map/while/body/eval_jaxpr/cond/branch_1_fun/dot_general | solution.py:84
  69.2 25.6 %while.46 = (s32[]{:T(128)}, bf16[512,256]{1,0:T(8,128)(2,1)S(1)}, s32[512]{0:T(512)S(1)}, f32[2048]{0:T(1024)S(1)}, f32[2048]{0:T(1024)S(1)}, /*index=5*/f32[20...) while((s32[]{:T(128)}, bf16[512,256]{1,0:T(8,128)(2,1)S(1)}, ...), condition=%wide.region_10.11_spmd.clone, body=%wide.region_5.10_spmd.clone.sunk | while | flops 558371328 | bytes 17304096 | solution.py:167
  69.2 1.5 collective-permute-start
  71.8 6.0 %collective-permute-done.1 = s32[512]{0:T(512)S(1)} collective-permute-done((s32[512]{0:T(512)S(1)}, s32[512]{0:T(512)S(1)}, u32[]{:S(2)}, u32[]{:S(2)}) %collective-permute-start.1) | collective-permute-done | bytes 2080 | tf_op jit(solution)/shard_map/while/body/eval_jaxpr/ppermute | solution.py:27
  79.7 5.3 %conditional.5 = ((f32[2048]{0:T(1024)S(1)}, f32[2048]{0:T(1024)S(1)}, f32[2048,128]{1,0:T(8,128)S(1)})) conditional(s32[]{:T(128)} %convert_element_type.75, (f32[2048]{0:T(1024)S(1)}, f32[2048]{0:T(1024)S(1)}, f32[2048,128]{1,0:T(8,128)S(1)}) %tuple.76, (s32[]{:T(128)}, s32[512]{0:T(512)S(1)}, s32[512]{0:T(512)S(1)}, s32[512]{0:T(512)S(1)}, ...), branch_computations={%region_6.6_spmd, %region_7.9_spmd} | conditional | flops 558371328 | bytes 15716388 | solution.py:99
  80.3 1.1 select_reduce_fusion.1
  81.5 1.6 fusion.20
  83.1 1.8 %convolution_add_fusion.1 = f32[2048,128]{1,0:T(8,128)S(1)} fusion(f32[2048,512]{0,1:T(8,128)S(1)} %get-tuple-element.582, f32[2048]{0:T(1024)S(1)} %max.5, s32[2048]{0:T(1024)S(1)} %eq.35, s32[2048]{0:T(1024)S(1)} %le.40, s32[512]{0:T(512)S(1)} %get-tuple-element.462, s32[512]{0:T(512)S(1)} %broadcast_add_fusion, f32[2048,128]{1,0:T(8,128)S(1)} %get-tuple-element.467, ...), kind=kOutput, calls=%fused_computation.25 | convolution fusion | flops 276299776 | bytes 6459392 | tf_op jit(solution)/shard_map/while/body/eval_jaxpr/while/body/eval_jaxpr/cond/branch_1_fun/dot_general | solution.py:84
  85.0 1.5 collective-permute-start
  87.2 5.6 %collective-permute-done.1 = s32[512]{0:T(512)S(1)} collective-permute-done((s32[512]{0:T(512)S(1)}, s32[512]{0:T(512)S(1)}, u32[]{:S(2)}, u32[]{:S(2)}) %collective-permute-start.1) | collective-permute-done | bytes 2080 | tf_op jit(solution)/shard_map/while/body/eval_jaxpr/ppermute | solution.py:27
  95.4 6.5 %convolution_convert_fusion = bf16[512,4096]{1,0:T(8,128)(2,1)} fusion(bf16[512,512]{1,0:T(8,128)(2,1)S(1)} %reshape.146, bf16[512,4096]{1,0:T(8,128)(2,1)} %param.14), kind=kOutput, calls=%fused_computation.48 | convolution fusion | flops 2149580800 | bytes 8912896 | tf_op jit(solution)/shard_map/dot_general | solution.py:169
  101.9 56.7 %reduce-scatter.2.cloned.1.call-done = bf16[512,512]{1,0:T(8,128)(2,1)} async-done(((bf16[512,4096]{1,0:T(8,128)(2,1)}), bf16[512,512]{1,0:T(8,128)(2,1)}) %reduce-scatter.2.cloned.1.call-update) | async-done | bytes 524304 | tf_op jit(solution)/shard_map/reduce_scatter | solution.py:170
  (70 shorter events, 10.4 us)
Async XLA Ops:
  6.5 41.2 %all-gather.3.cloned.1.call-start = ((), (), s32[]{:S(2)}) async-start(), calls=%async_computation.1 | async-start | bytes 4718592 | tf_op jit(solution)/shard_map/all_gather | solution.py:113
  7.3 151.4 %reduce-scatter.2.cloned.1.call-start = ((), (), s32[]{:S(2)}) async-start(), calls=%async_computation.2 | async-start | bytes 4718592 | tf_op jit(solution)/shard_map/reduce_scatter | solution.py:170
  16.9 0.6 copy-start.3
  16.9 39.9 %copy-start.5 = (f32[512]{0:T(512)}, f32[512]{0:T(512)S(1)}, u32[]{:S(2)}) copy-start(f32[512]{0:T(512)S(1)} %get-tuple-element.592) | copy-start | bytes 6148
  22.6 1.8 %copy-start.6 = (f32[64]{0:T(128)}, f32[64]{0:T(128)S(1)}, u32[]{:S(2)}) copy-start(f32[64]{0:T(128)S(1)} %negate_power_fusion) | copy-start | bytes 772
  47.8 3.4 %copy-start = (bf16[512,4096]{1,0:T(8,128)(2,1)S(1)}, bf16[512,4096]{1,0:T(8,128)(2,1)}, u32[]{:S(2)}) copy-start(bf16[512,4096]{1,0:T(8,128)(2,1)} %all-gather.3.cloned.1.call-done) | copy-start | bytes 12582916
  60.6 3.0 %copy-start.2 = (s32[512]{0:T(512)S(1)}, s32[512]{0:T(512)}, u32[]{:S(2)}) copy-start(s32[512]{0:T(512)} %param.15) | copy-start | bytes 6148
  60.6 3.0 %copy-start.4 = (s32[512]{0:T(512)S(1)}, s32[512]{0:T(512)}, u32[]{:S(2)}) copy-start(s32[512]{0:T(512)} %copy-done.3) | copy-start | bytes 6148
  63.6 5.6 %copy-start.1 = (bf16[512,256]{1,0:T(8,128)(2,1)S(1)}, bf16[512,256]{1,0:T(8,128)(2,1)}, u32[]{:S(2)}) copy-start(bf16[512,256]{1,0:T(8,128)(2,1)} %copy.9) | copy-start | bytes 786436
  63.6 5.6 %copy-start.7 = (s32[512]{0:T(512)S(1)}, s32[512]{0:T(512)}, u32[]{:S(2)}) copy-start(s32[512]{0:T(512)} %copy.26) | copy-start | bytes 6148
  69.2 10.5 %collective-permute-start = (bf16[512,256]{1,0:T(8,128)(2,1)S(1)}, bf16[512,256]{1,0:T(8,128)(2,1)S(1)}, u32[]{:S(2)}, u32[]{:S(2)}) collective-permute-start(bf16[512,256]{1,0:T(8,128)(2,1)S(1)} %get-tuple-element.702), channel_id=1, source_target_pairs={{24,0},{0,8},{8,16},{16,24},{25,1},{1,9},{9,17},{17,25},{26,2},{2,... | collective-permute-start | bytes 786440 | tf_op jit(solution)/shard_map/while/body/eval_jaxpr/ppermute | solution.py:27
  70.7 7.0 %collective-permute-start.1 = (s32[512]{0:T(512)S(1)}, s32[512]{0:T(512)S(1)}, u32[]{:S(2)}, u32[]{:S(2)}) collective-permute-start(s32[512]{0:T(512)S(1)} %get-tuple-element.703), channel_id=1, source_target_pairs={{24,0},{0,8},{8,16},{16,24},{25,1},{1,9},{9,17},{17,25},{26,2},{2,... | collective-permute-start | bytes 6152 | tf_op jit(solution)/shard_map/while/body/eval_jaxpr/ppermute | solution.py:27
  85.0 9.7 %collective-permute-start = (bf16[512,256]{1,0:T(8,128)(2,1)S(1)}, bf16[512,256]{1,0:T(8,128)(2,1)S(1)}, u32[]{:S(2)}, u32[]{:S(2)}) collective-permute-start(bf16[512,256]{1,0:T(8,128)(2,1)S(1)} %get-tuple-element.702), channel_id=1, source_target_pairs={{24,0},{0,8},{8,16},{16,24},{25,1},{1,9},{9,17},{17,25},{26,2},{2,... | collective-permute-start | bytes 786440 | tf_op jit(solution)/shard_map/while/body/eval_jaxpr/ppermute | solution.py:27
  86.5 6.2 %collective-permute-start.1 = (s32[512]{0:T(512)S(1)}, s32[512]{0:T(512)S(1)}, u32[]{:S(2)}, u32[]{:S(2)}) collective-permute-start(s32[512]{0:T(512)S(1)} %get-tuple-element.703), channel_id=1, source_target_pairs={{24,0},{0,8},{8,16},{16,24},{25,1},{1,9},{9,17},{17,25},{26,2},{2,... | collective-permute-start | bytes 6152 | tf_op jit(solution)/shard_map/while/body/eval_jaxpr/ppermute | solution.py:27
Sparse Core Ops, SparseCore 0:
  9.2 38.4 all-gather.2
  102.1 56.5 reduce-scatter.1
where the time goes:
time: 168 us; the launch traced here: 165 us
  waiting for transfers between devices  92.4 us (55%)
  matrix products  18 us (11%)
  between operations  15.5 us (9%)
  other arithmetic  11.9 us (7%)
  local copies, waits for them, and re-layouts  10.9 us (6%)
  blocking collectives  8.89 us (5%)
  loops' own time  4.16 us (2%)
  starting transfers between devices  3.66 us (2%)
    reduce_scatter x1, waiting for transfers between devices, body(): lax.psum_scatter(partial_products.astype(jnp.bfloat16), ('head', 'grp'),...  56.7 us
    all_gather x1, waiting for transfers between devices, body(): lax.all_gather(tokens, ('head', 'grp'), axis=1, tiled=True)  23.3 us
    ppermute x4, waiting for transfers between devices, passed_along(): return lax.ppermute(block, axis, route)  11.6 us
    all_gather x1, blocking collectives, body(): lax.all_gather(norm_gain, ('head', 'grp'), axis=0, tiled=True)  8.89 us
    dot_general x1, matrix products, body(): jnp.dot(heads, out_weight, preferred_element_type=jnp.float32)  6.49 us
    dot_general x1, matrix products, body(): jnp.dot(normed_input, query_key_value_weight, preferred_element_type=jnp....  5.61 us
    unnamed x21, local copies, waits for them, and re-layouts  4.78 us
    another operation x1, loops' own time, body(): lax.fori_loop(1, reach + 1, advance, ((key_value, doc_ids), first_states))  3.79 us
  transfers between devices with their start and end apart: 6, of which 4 were waited for; matrix products, arithmetic and copies ran while one was open for 4% of the time, Pallas kernels for 0%

commit v1 on v0

v1 whole, which is shorter than its diff:
```python
import functools

import jax
import jax.numpy as jnp
import numpy as np
from jax import lax
from jax.experimental import pallas as pl
from jax.experimental.pallas import tpu as pltpu
from jax.sharding import PartitionSpec as P

QUERY_HEADS = 32
KEY_VALUE_HEADS = 8
HEAD_SIZE = 128
GROUP = QUERY_HEADS // KEY_VALUE_HEADS

epsilon = 1e-05
theta = 500000.0
floor_score = -1e30
HEADER = 16
CHUNKS = 4
MESH = pl.DeviceIdType.MESH


def kernel(
    size, tokens_hbm, gain_ref, wqkv_hbm, wout_hbm, docs_ref, local_ref, base_ref, out_ref,
    gath, wqkv, wout, queries, kvs, mixed, owners, highs, totals, accums,
    sib_out, sib_in, part, x_out, x_in,
    load_sem, ag_send, ag_recv, kv_send, kv_recv, sib_send, sib_recv, x_send, x_recv,
):
    tok_size, reach = size, size // 2
    length, width = tokens_hbm.shape
    blocks = gath.shape[0]
    chips = blocks // 2
    rows = length // CHUNKS
    t = lax.axis_index("tok")
    h = lax.axis_index("head")
    c = lax.axis_index("grp")
    hx = h + 1 - 2 * (h % 2)
    hy = h + 2 - 4 * ((h // 2) % 2)
    ha = hx * (1 - c) + hy * c
    hb = hy * (1 - c) + hx * c
    hd = hx + hy - h
    s = 1 - c
    me = h * 2 + c
    to_a, to_b, to_sib = {"head": ha}, {"head": hb}, {"grp": s}

    load_tokens = pltpu.make_async_copy(
        tokens_hbm, gath.at[me, pl.ds(HEADER, length)], load_sem.at[0]
    )
    load_tokens.start()
    load_wqkv = pltpu.make_async_copy(wqkv_hbm, wqkv, load_sem.at[1])
    load_wqkv.start()
    load_wout = [
        pltpu.make_async_copy(
            wout_hbm.at[:, pl.ds(d * width, width)], wout.at[d], load_sem.at[2 + d]
        )
        for d in range(blocks)
    ]
    for load in load_wout:
        load.start()

    barrier = pltpu.get_barrier_semaphore()
    for device in (to_a, to_b, to_sib):
        pl.semaphore_signal(barrier, inc=1, device_id=device, device_id_type=MESH)
    for step in range(1, reach + 1):

        @pl.when(t + step < tok_size)
        def _():
            pl.semaphore_signal(barrier, inc=1, device_id={"tok": t + step}, device_id_type=MESH)

        @pl.when(t >= step)
        def _():
            pl.semaphore_signal(barrier, inc=1, device_id={"tok": t - step}, device_id_type=MESH)

    gath[me, 0:HEADER, :] = jnp.broadcast_to(
        gain_ref[...].astype(jnp.float32), (HEADER, width)
    ).astype(jnp.bfloat16)
    docs = docs_ref[...].astype(jnp.float32)
    pair = 2 * HEAD_SIZE
    row_index = lax.broadcasted_iota(jnp.int32, (HEADER, pair), 0)
    packed = jnp.zeros((HEADER, pair), jnp.float32)
    for i in range(length // pair):
        packed = jnp.where(row_index == i, docs[:, i * pair : (i + 1) * pair], packed)
    kvs[0, length : length + HEADER, :] = packed.astype(jnp.bfloat16)

    later = jnp.minimum(reach, tok_size - 1 - t)
    earlier = jnp.minimum(reach, t)
    pl.semaphore_wait(barrier, 3 + later + earlier)

    sent = []

    def piece(d, r):
        if r == 0:
            return gath.at[d, pl.ds(0, HEADER + rows)]
        return gath.at[d, pl.ds(HEADER + r * rows, rows)]

    kinds = (
        (me, to_a, ha * 2 + c),
        (me, to_b, hb * 2 + c),
        (ha * 2 + c, to_b, hd * 2 + c),
        (me, to_sib, h * 2 + s),
        (ha * 2 + c, to_sib, hb * 2 + s),
        (hb * 2 + c, to_sib, ha * 2 + s),
        (hd * 2 + c, to_sib, hd * 2 + s),
    )

    def ag_copy(kind, r, block):
        return pltpu.make_async_remote_copy(
            src_ref=piece(block, r),
            dst_ref=piece(block, r),
            send_sem=ag_send.at[kind, r],
            recv_sem=ag_recv.at[kind, r],
            device_id=kinds[kind][1],
            device_id_type=MESH,
        )

    def go(kind, r):
        copy = ag_copy(kind, r, kinds[kind][0])
        copy.start()
        sent.append(copy)

    def got(kind, r):
        ag_copy(kind, r, kinds[kind][2]).wait_recv()

    def own(r):
        for kind in (0, 1, 3):
            go(kind, r)

    def relay(r):
        got(0, r)
        go(2, r)
        go(4, r)
        got(1, r)
        go(5, r)

    base = base_ref[t]
    base_cos, base_sin = base[0:1, :], base[1:2, :]

    def project(r):
        where = pl.ds(HEADER + r * rows, rows)

        def square(d, held):
            x = gath[d, where, :].astype(jnp.float32)
            return held + jnp.sum(x * x, axis=1, keepdims=True)

        squares = lax.fori_loop(0, blocks, square, jnp.zeros((rows, 1), jnp.float32))
        inverse = lax.rsqrt(squares * (1.0 / (blocks * width)) + epsilon)
        mixed[...] = jnp.zeros_like(mixed)

        def multiply(d, _):
            gain = gath[d, 0:HEADER, :].astype(jnp.float32)[0:1, :]
            x = gath[d, where, :].astype(jnp.float32)
            normed = (x * inverse * gain).astype(jnp.bfloat16)
            mixed[...] += jnp.dot(normed, wqkv[d], preferred_element_type=jnp.float32)
            return 0

        lax.fori_loop(0, blocks, multiply, 0)
        span = slice(r * rows, (r + 1) * rows)
        local_cos, local_sin = local_ref[0, span, :], local_ref[1, span, :]
        cosine = local_cos * base_cos - local_sin * base_sin
        sine = local_sin * base_cos + local_cos * base_sin

        def turned(j):
            v = mixed[:, j * HEAD_SIZE : (j + 1) * HEAD_SIZE]
            return (v * cosine + pltpu.roll(v, HEAD_SIZE // 2, 1) * sine).astype(jnp.bfloat16)

        for j in range(GROUP):
            queries[r, j * rows : (j + 1) * rows, :] = turned(j)
        kvs[0, span, 0:HEAD_SIZE] = turned(GROUP)
        kvs[0, span, HEAD_SIZE:] = mixed[:, (GROUP + 1) * HEAD_SIZE :].astype(jnp.bfloat16)

    def kv_piece(slot, r):
        return kvs.at[slot, pl.ds(r * rows, rows + (HEADER if r == CHUNKS - 1 else 0))]

    def kv_copy(step, r, source):
        return pltpu.make_async_remote_copy(
            src_ref=kv_piece(source, r),
            dst_ref=kv_piece(step, r),
            send_sem=kv_send.at[step - 1, r],
            recv_sem=kv_recv.at[step - 1, r],
            device_id={"tok": (t + step) % tok_size},
            device_id_type=MESH,
        )

    power = HEAD_SIZE ** (-0.5) * float(np.log2(np.e))

    def key_docs(slot):
        held = kvs[slot, length : length + HEADER, :].astype(jnp.float32)
        return jnp.concatenate([held[i : i + 1, :] for i in range(length // pair)], axis=1)

    for r in range(CHUNKS):
        line = docs[:, r * rows : (r + 1) * rows]
        owners[r] = jnp.transpose(jnp.broadcast_to(line, (rows, rows)))[:, 0:1]

    def attend(r, slot, first):
        count = (r + 1) * rows if first else length
        q = queries[r]
        k = kvs[slot, 0:count, 0:HEAD_SIZE]
        v = kvs[slot, 0:count, HEAD_SIZE:]
        scores = lax.dot_general(
            q, k, (((1,), (1,)), ((), ())), preferred_element_type=jnp.float32
        )
        mask = key_docs(slot)[:, 0:count] == owners[r]
        if first:
            mask = mask & (
                lax.broadcasted_iota(jnp.int32, (rows, count), 1)
                <= lax.broadcasted_iota(jnp.int32, (rows, count), 0) + r * rows
            )
        scores = jnp.where(mask[None], scores.reshape(GROUP, rows, count), floor_score)
        scores = scores.reshape(GROUP * rows, count)
        high = jnp.max(scores, axis=1, keepdims=True)
        if not first:
            high = jnp.maximum(high, highs[r])
        weights = jnp.exp2((scores - high) * power)
        total = jnp.sum(weights, axis=1, keepdims=True)
        summed = jnp.dot(weights.astype(jnp.bfloat16), v, preferred_element_type=jnp.float32)
        if not first:
            fade = jnp.exp2((highs[r] - high) * power)
            total = total + totals[r] * fade
            summed = summed + accums[r] * fade
        highs[r] = high
        totals[r] = total
        accums[r] = summed

    load_tokens.wait()
    own(0)
    own(1)
    relay(0)
    load_wqkv.wait()
    for r in range(CHUNKS):
        if r + 2 < CHUNKS:
            own(r + 2)
        if r + 1 < CHUNKS:
            relay(r + 1)
        got(2, r)
        go(6, r)
        for kind in (3, 4, 5, 6):
            got(kind, r)
        project(r)

        @pl.loop(1, later + 1)
        def _(step):
            kv_copy(step, r, 0).start()

        attend(r, 0, True)

    def sib_copy(r):
        return pltpu.make_async_remote_copy(
            src_ref=sib_out.at[r], dst_ref=sib_in.at[r], send_sem=sib_send.at[r],
            recv_sem=sib_recv.at[r], device_id=to_sib, device_id_type=MESH,
        )

    def x_copy(r, i):
        return pltpu.make_async_remote_copy(
            src_ref=x_out.at[r, i], dst_ref=x_in.at[r, i], send_sem=x_send.at[r, i],
            recv_sem=x_recv.at[r, i], device_id=to_a if i == 2 else to_b, device_id_type=MESH,
        )

    def start(copy):
        copy.start()
        sent.append(copy)

    def project_out(r):
        normal = (accums[r] / totals[r]).astype(jnp.bfloat16)
        heads = jnp.concatenate([normal[j * rows : (j + 1) * rows] for j in range(GROUP)], axis=1)

        def for_sib(q, _):
            sib_out[r, q] = jnp.dot(
                heads, wout[q * 2 + s], preferred_element_type=jnp.float32
            ).astype(jnp.bfloat16)
            return 0

        lax.fori_loop(0, chips, for_sib, 0)
        start(sib_copy(r))

        def for_own(q, _):
            part[r, q] = jnp.dot(heads, wout[q * 2 + c], preferred_element_type=jnp.float32)
            return 0

        lax.fori_loop(0, chips, for_own, 0)

    def both(r, q):
        return part[r, q] + sib_in[r, q].astype(jnp.float32)

    def stage_one(r):
        sib_copy(r).wait_recv()
        for i, q in enumerate((hd, hb)):
            x_out[r, i] = both(r, q).astype(jnp.bfloat16)
            start(x_copy(r, i))

    def stage_two(r):
        x_copy(r, 0).wait_recv()
        x_out[r, 2] = (both(r, ha) + x_in[r, 0].astype(jnp.float32)).astype(jnp.bfloat16)
        start(x_copy(r, 2))

    def stage_three(r):
        x_copy(r, 1).wait_recv()
        x_copy(r, 2).wait_recv()
        out_ref[r * rows : (r + 1) * rows, :] = (
            both(r, h) + x_in[r, 1].astype(jnp.float32) + x_in[r, 2].astype(jnp.float32)
        ).astype(jnp.bfloat16)

    @pl.loop(1, jnp.minimum(reach - 1, t) + 1)
    def _(step):
        for r in range(CHUNKS):
            kv_copy(step, r, step).wait_recv()

        @pl.loop(0, CHUNKS)
        def _(r):
            attend(r, step, False)

    @pl.when(t >= reach)
    def _():
        for r in range(CHUNKS):
            kv_copy(reach, r, reach).wait_recv()

    for load in load_wout:
        load.wait()
    for r in range(CHUNKS + 3):
        if r < CHUNKS:

            @pl.when(t >= reach)
            def _():
                attend(r, reach, False)

            project_out(r)
        if 0 <= r - 1 < CHUNKS:
            stage_one(r - 1)
        if 0 <= r - 2 < CHUNKS:
            stage_two(r - 2)
        if 0 <= r - 3 < CHUNKS:
            stage_three(r - 3)

    for copy in sent:
        copy.wait_send()
    @pl.loop(1, later + 1)
    def _(step):
        for r in range(CHUNKS):
            kv_copy(step, r, 0).wait_send()


def tables(length, tok_size):
    half = HEAD_SIZE // 2
    inverse = theta ** (-np.arange(half, dtype=np.float64) * (2.0 / HEAD_SIZE))

    def pair(positions):
        angles = positions[:, None] * inverse[None, :]
        cosine, sine = np.cos(angles), np.sin(angles)
        return np.stack(
            [np.concatenate([cosine, cosine], 1), np.concatenate([-sine, sine], 1)]
        ).astype(np.float32)

    local = pair(np.arange(length, dtype=np.float64))
    base = pair(np.arange(tok_size, dtype=np.float64) * length).transpose(1, 0, 2)
    return jnp.asarray(local), jnp.asarray(base)


def body(mesh_shape, tokens, norm_gain, query_key_value_weight, out_weight, doc_ids):
    tok_size = mesh_shape["tok"]
    blocks = mesh_shape["head"] * mesh_shape["grp"]
    chips = blocks // 2
    reach = tok_size // 2
    length, width = tokens.shape
    rows = length // CHUNKS
    columns = query_key_value_weight.shape[1]
    local, base = tables(length, tok_size)
    bf16, f32 = jnp.bfloat16, jnp.float32
    vmem = pl.BlockSpec(memory_space=pltpu.VMEM)
    hbm = pl.BlockSpec(memory_space=pl.ANY)
    dma = pltpu.SemaphoreType.DMA
    return pl.pallas_call(
        functools.partial(kernel, tok_size),
        out_shape=jax.ShapeDtypeStruct((length, width), bf16),
        in_specs=[hbm, vmem, hbm, hbm, vmem, vmem, vmem],
        out_specs=vmem,
        scratch_shapes=[
            pltpu.VMEM((blocks, HEADER + length, width), bf16),
            pltpu.VMEM((blocks, width, columns), bf16),
            pltpu.VMEM((blocks, out_weight.shape[0], width), bf16),
            pltpu.VMEM((CHUNKS, GROUP * rows, HEAD_SIZE), bf16),
            pltpu.VMEM((1 + reach, length + HEADER, 2 * HEAD_SIZE), bf16),
            pltpu.VMEM((rows, columns), f32),
            pltpu.VMEM((CHUNKS, rows, 1), f32),
            pltpu.VMEM((CHUNKS, GROUP * rows, 1), f32),
            pltpu.VMEM((CHUNKS, GROUP * rows, 1), f32),
            pltpu.VMEM((CHUNKS, GROUP * rows, HEAD_SIZE), f32),
            pltpu.VMEM((CHUNKS, chips, rows, width), bf16),
            pltpu.VMEM((CHUNKS, chips, rows, width), bf16),
            pltpu.VMEM((CHUNKS, chips, rows, width), f32),
            pltpu.VMEM((CHUNKS, 3, rows, width), bf16),
            pltpu.VMEM((CHUNKS, 3, rows, width), bf16),
            dma((2 + blocks,)),
            dma((7, CHUNKS)),
            dma((7, CHUNKS)),
            dma((reach, CHUNKS)),
            dma((reach, CHUNKS)),
            dma((CHUNKS,)),
            dma((CHUNKS,)),
            dma((CHUNKS, 3)),
            dma((CHUNKS, 3)),
        ],
        compiler_params=pltpu.CompilerParams(
            collective_id=0, has_side_effects=True, vmem_limit_bytes=58 * 2**20
        ),
    )(
        tokens,
        norm_gain.reshape(1, width),
        query_key_value_weight.reshape(blocks, width, columns),
        out_weight,
        doc_ids.reshape(1, length),
        local,
        base,
    )


def solution(mesh):
    return jax.shard_map(
        functools.partial(body, dict(mesh.shape)),
        mesh=mesh,
        in_specs=(
            P("tok", ("head", "grp")),
            P(("head", "grp")),
            P(None, ("head", "grp")),
            P(("head", "grp"), None),
            P("tok"),
        ),
        out_specs=P("tok", ("head", "grp")),
        check_vma=False,
    )
```

time: 168 us -> 77.3 us (0.46); the launches traced: 165 us -> 77.1 us
  waiting for transfers between devices: 92.4 us -> 0 us
  Pallas kernels: 0 us -> 73.9 us
  matrix products: 18 us -> 0 us
  between operations: 15.5 us -> 0.01 us
  other arithmetic: 11.9 us -> 0 us
  blocking collectives: 8.89 us -> 0 us
  local copies, waits for them, and re-layouts: 10.9 us -> 3.13 us
  loops' own time: 4.16 us -> 0 us
  starting transfers between devices: 3.66 us -> 0 us
    pallas_call x0 -> x1, Pallas kernels: none -> 73.9 us  [body(): pl.pallas_call(functools.partial(kernel, tok_size), out_shape=jax.ShapeDt...]
    reduce_scatter x1 -> x0, waiting for transfers between devices: 56.7 us -> none  [body(): lax.psum_scatter(partial_products.astype(jnp.bfloat16), ('head', 'grp'),...]
    all_gather x1 -> x0, waiting for transfers between devices: 23.3 us -> none  [body(): lax.all_gather(tokens, ('head', 'grp'), axis=1, tiled=True)]
    dot_general x6 -> x0, matrix products: 18 us -> none  [the longest x1 6.49 us: body(): jnp.dot(heads, out_weight, preferred_element_type=jnp.float32)]
    ppermute x4 -> x0, waiting for transfers between devices: 11.6 us -> none  [passed_along(): return lax.ppermute(block, axis, route)]
    all_gather x1 -> x0, blocking collectives: 8.89 us -> none  [body(): lax.all_gather(norm_gain, ('head', 'grp'), axis=0, tiled=True)]
    reduce_sum x3 -> x0, other arithmetic: 6.42 us -> none  [the longest x1 3.23 us: body(): jnp.mean(floats * floats, axis=1, keepdims=True) + epsilon]
    another operation x4 -> x0, loops' own time: 4.16 us -> none  [the longest x1 3.79 us: body(): lax.fori_loop(1, reach + 1, advance, ((key_value, doc_ids), first_states))]
  transfers between devices with their start and end apart: 6 -> 0, of which waited for: 4 -> 0; matrix products, arithmetic and copies ran while one was open for 4% -> 0% of each run, Pallas kernels for 0% -> 0%
where the time goes in v1:
time: 77.3 us; the launch traced here: 77.1 us
  Pallas kernels  73.9 us (96%)
  local copies, waits for them, and re-layouts  3.13 us (4%)
    pallas_call x1, Pallas kernels, body(): pl.pallas_call(functools.partial(kernel, tok_size), out_shape=jax.ShapeDt...  73.9 us
    unnamed x1, local copies, waits for them, and re-layouts  1.87 us

profile of v1, /device:TPU:16, one launch (start us, length us, event | category | flops | bytes accessed | tf_op | source)
XLA Modules:
  0.0 77.1 jit_solution(13242329417385121471)
XLA Ops:
  0.0 1.3 %reshape.9.gain_ref = bf16[1,512]{1,0:T(2,128)(2,1)} reshape(bf16[512]{0:T(512)(128)(2,1)} %param.8) | data formatting | bytes 2048 | tf_op jit(solution)/shard_map/reshape | solution.py:407
  1.3 73.9 %shard_map.73 = bf16[512,512]{1,0:T(8,128)(2,1)} custom-call(bf16[512,512]{1,0:T(8,128)(2,1)} %tokens_hbm.1, bf16[1,512]{1,0:T(2,128)(2,1)} %reshape.9.gain_ref, bf16[8,512,768]{2,1,0:T(8,128)(2,1)} %bitcast.2, bf16[512,4096]{1,0:T(8,128)(2,1)} %wout_hbm.1, s32[1,512]{1,0:T(1,128)} %bitcast.3, f32[2,512,128]{2,1,0:T(8,128)} %constant.4.clone.local_ref, ...), custom_call_target="tpu_custom_call" | custom-call | tf_op jit(solution)/shard_map/pallas_call | solution.py:371
  75.2 1.9 %copy.9 = bf16[512,512]{1,0:T(8,128)(2,1)} copy(bf16[512,512]{1,0:T(8,128)(2,1)} %shard_map.73) | data formatting | bytes 1048576

commit v2 on v1

--- a/solution.py
+++ b/solution.py
@@ -62,18 +62,16 @@
     barrier = pltpu.get_barrier_semaphore()
     for device in (to_a, to_b, to_sib):
         pl.semaphore_signal(barrier, inc=1, device_id=device, device_id_type=MESH)
-    for step in range(1, reach + 1):
-
-        @pl.when(t + step < tok_size)
-        def _():
-            pl.semaphore_signal(barrier, inc=1, device_id={"tok": t + step}, device_id_type=MESH)
-
-        @pl.when(t >= step)
-        def _():
-            pl.semaphore_signal(barrier, inc=1, device_id={"tok": t - step}, device_id_type=MESH)
+    @pl.when(t + 1 < tok_size)
+    def _():
+        pl.semaphore_signal(barrier, inc=1, device_id={"tok": t + 1}, device_id_type=MESH)
+
+    @pl.when(t >= 1)
+    def _():
+        pl.semaphore_signal(barrier, inc=1, device_id={"tok": t - 1}, device_id_type=MESH)
 
     gath[me, 0:HEADER, :] = jnp.broadcast_to(
-        gain_ref[...].astype(jnp.float32), (HEADER, width)
+        gain_ref[...].astype(jnp.float32).reshape(1, width), (HEADER, width)
     ).astype(jnp.bfloat16)
     docs = docs_ref[...].astype(jnp.float32)
     pair = 2 * HEAD_SIZE
@@ -83,8 +81,8 @@
         packed = jnp.where(row_index == i, docs[:, i * pair : (i + 1) * pair], packed)
     kvs[0, length : length + HEADER, :] = packed.astype(jnp.bfloat16)
 
-    later = jnp.minimum(reach, tok_size - 1 - t)
-    earlier = jnp.minimum(reach, t)
+    later = jnp.minimum(1, tok_size - 1 - t)
+    earlier = jnp.minimum(1, t)
     pl.semaphore_wait(barrier, 3 + later + earlier)
 
     sent = []
@@ -143,7 +141,7 @@
             x = gath[d, where, :].astype(jnp.float32)
             return held + jnp.sum(x * x, axis=1, keepdims=True)
 
-        squares = lax.fori_loop(0, blocks, square, jnp.zeros((rows, 1), jnp.float32))
+        squares = lax.fori_loop(0, blocks, square, jnp.zeros((rows, 1), jnp.float32), unroll=True)
         inverse = lax.rsqrt(squares * (1.0 / (blocks * width)) + epsilon)
         mixed[...] = jnp.zeros_like(mixed)
 
@@ -154,7 +152,7 @@
             mixed[...] += jnp.dot(normed, wqkv[d], preferred_element_type=jnp.float32)
             return 0
 
-        lax.fori_loop(0, blocks, multiply, 0)
+        lax.fori_loop(0, blocks, multiply, 0, unroll=True)
         span = slice(r * rows, (r + 1) * rows)
         local_cos, local_sin = local_ref[0, span, :], local_ref[1, span, :]
         cosine = local_cos * base_cos - local_sin * base_sin
@@ -172,15 +170,26 @@
     def kv_piece(slot, r):
         return kvs.at[slot, pl.ds(r * rows, rows + (HEADER if r == CHUNKS - 1 else 0))]
 
-    def kv_copy(step, r, source):
+    def kv_copy(step, r):
         return pltpu.make_async_remote_copy(
-            src_ref=kv_piece(source, r),
+            src_ref=kv_piece(step - 1, r),
             dst_ref=kv_piece(step, r),
             send_sem=kv_send.at[step - 1, r],
             recv_sem=kv_recv.at[step - 1, r],
-            device_id={"tok": (t + step) % tok_size},
+            device_id={"tok": (t + 1) % tok_size},
             device_id_type=MESH,
         )
+
+    def relay_kv(step, r):
+        @pl.when(t >= step)
+        def _():
+            kv_copy(step, r).wait_recv()
+
+        if not isinstance(step, int) or step < reach:
+
+            @pl.when((t >= step) & (t + 1 < tok_size))
+            def _():
+                kv_copy(step + 1, r).start()
 
     power = HEAD_SIZE ** (-0.5) * float(np.log2(np.e))
 
@@ -188,9 +197,10 @@
         held = kvs[slot, length : length + HEADER, :].astype(jnp.float32)
         return jnp.concatenate([held[i : i + 1, :] for i in range(length // pair)], axis=1)
 
-    for r in range(CHUNKS):
-        line = docs[:, r * rows : (r + 1) * rows]
-        owners[r] = jnp.transpose(jnp.broadcast_to(line, (rows, rows)))[:, 0:1]
+    for i in range(length // HEAD_SIZE):
+        line = docs[:, i * HEAD_SIZE : (i + 1) * HEAD_SIZE]
+        square_of = jnp.transpose(jnp.broadcast_to(line, (HEAD_SIZE, HEAD_SIZE)))
+        owners[i * HEAD_SIZE : (i + 1) * HEAD_SIZE, :] = square_of[:, 0:1]
 
     def attend(r, slot, first):
         count = (r + 1) * rows if first else length
@@ -200,7 +210,7 @@
         scores = lax.dot_general(
             q, k, (((1,), (1,)), ((), ())), preferred_element_type=jnp.float32
         )
-        mask = key_docs(slot)[:, 0:count] == owners[r]
+        mask = key_docs(slot)[:, 0:count] == owners[pl.ds(r * rows, rows), :]
         if first:
             mask = mask & (
                 lax.broadcasted_iota(jnp.int32, (rows, count), 1)
@@ -238,9 +248,12 @@
             got(kind, r)
         project(r)
 
-        @pl.loop(1, later + 1)
-        def _(step):
-            kv_copy(step, r, 0).start()
+        @pl.when(t + 1 < tok_size)
+        def _():
+            kv_copy(1, r).start()
+
+        if r >= 1:
+            relay_kv(1, r - 1)
 
         attend(r, 0, True)
 
@@ -300,19 +313,24 @@
             both(r, h) + x_in[r, 1].astype(jnp.float32) + x_in[r, 2].astype(jnp.float32)
         ).astype(jnp.bfloat16)
 
-    @pl.loop(1, jnp.minimum(reach - 1, t) + 1)
+    relay_kv(1, CHUNKS - 1)
+
+    @pl.loop(1, reach)
     def _(step):
+        @pl.when(step >= 2)
+        def _():
+            for r in range(CHUNKS):
+                relay_kv(step, r)
+
+        @pl.when(t >= step)
+        def _():
+            @pl.loop(0, CHUNKS)
+            def _(r):
+                attend(r, step, False)
+
+    if reach >= 2:
         for r in range(CHUNKS):
-            kv_copy(step, r, step).wait_recv()
-
-        @pl.loop(0, CHUNKS)
-        def _(r):
-            attend(r, step, False)
-
-    @pl.when(t >= reach)
-    def _():
-        for r in range(CHUNKS):
-            kv_copy(reach, r, reach).wait_recv()
+            relay_kv(reach, r)
 
     for load in load_wout:
         load.wait()
@@ -333,10 +351,12 @@
 
     for copy in sent:
         copy.wait_send()
-    @pl.loop(1, later + 1)
+    @pl.loop(1, reach + 1)
     def _(step):
-        for r in range(CHUNKS):
-            kv_copy(step, r, 0).wait_send()
+        @pl.when((t >= step - 1) & (t + 1 < tok_size))
+        def _():
+            for r in range(CHUNKS):
+                kv_copy(step, r).wait_send()
 
 
 def tables(length, tok_size):
@@ -380,7 +400,7 @@
             pltpu.VMEM((CHUNKS, GROUP * rows, HEAD_SIZE), bf16),
             pltpu.VMEM((1 + reach, length + HEADER, 2 * HEAD_SIZE), bf16),
             pltpu.VMEM((rows, columns), f32),
-            pltpu.VMEM((CHUNKS, rows, 1), f32),
+            pltpu.VMEM((length, 1), f32),
             pltpu.VMEM((CHUNKS, GROUP * rows, 1), f32),
             pltpu.VMEM((CHUNKS, GROUP * rows, 1), f32),
             pltpu.VMEM((CHUNKS, GROUP * rows, HEAD_SIZE), f32),
@@ -404,7 +424,7 @@
         ),
     )(
         tokens,
-        norm_gain.reshape(1, width),
+        norm_gain,
         query_key_value_weight.reshape(blocks, width, columns),
         out_weight,
         doc_ids.reshape(1, length),

time: 77.3 us -> 69.2 us (0.90)
  Pallas kernels: 73.9 us -> 67.2 us
  local copies, waits for them, and re-layouts: 3.13 us -> 1.87 us
    pallas_call x1, Pallas kernels: 73.9 us -> 67.2 us  [body(): pl.pallas_call(functools.partial(kernel, tok_size), out_shape=jax.ShapeDt...]
    reshape x1 -> x0, local copies, waits for them, and re-layouts: 1.26 us -> none  [body(): norm_gain.reshape(1, width)]
where the time goes in v2:
time: 69.2 us; the launch traced here: 69.1 us
  Pallas kernels  67.2 us (97%)
  local copies, waits for them, and re-layouts  1.87 us (3%)
    pallas_call x1, Pallas kernels, body(): pl.pallas_call(functools.partial(kernel, tok_size), out_shape=jax.ShapeDt...  67.2 us
    unnamed x1, local copies, waits for them, and re-layouts  1.87 us

profile of v2, /device:TPU:16, one launch (start us, length us, event | category | flops | bytes accessed | tf_op | source)
XLA Modules:
  0.0 69.1 jit_solution(1912784091440056006)
XLA Ops:
  0.0 67.2 %shard_map.73 = bf16[512,512]{1,0:T(8,128)(2,1)} custom-call(bf16[512,512]{1,0:T(8,128)(2,1)} %tokens_hbm.1, bf16[512]{0:T(512)(128)(2,1)} %gain_ref.1, bf16[8,512,768]{2,1,0:T(8,128)(2,1)} %bitcast.2, bf16[512,4096]{1,0:T(8,128)(2,1)} %wout_hbm.1, s32[1,512]{1,0:T(1,128)} %bitcast.3, f32[2,512,128]{2,1,0:T(8,128)} %constant.4.clone.local_ref, ...), custom_call_target="tpu_custom_call" | custom-call | tf_op jit(solution)/shard_map/pallas_call | solution.py:391
  67.2 1.9 %copy.9 = bf16[512,512]{1,0:T(8,128)(2,1)} copy(bf16[512,512]{1,0:T(8,128)(2,1)} %shard_map.73) | data formatting | bytes 1048576

commit v3 on v2

--- a/solution.py
+++ b/solution.py
@@ -283,14 +283,14 @@
             ).astype(jnp.bfloat16)
             return 0
 
-        lax.fori_loop(0, chips, for_sib, 0)
+        lax.fori_loop(0, chips, for_sib, 0, unroll=True)
         start(sib_copy(r))
 
         def for_own(q, _):
             part[r, q] = jnp.dot(heads, wout[q * 2 + c], preferred_element_type=jnp.float32)
             return 0
 
-        lax.fori_loop(0, chips, for_own, 0)
+        lax.fori_loop(0, chips, for_own, 0, unroll=True)
 
     def both(r, q):
         return part[r, q] + sib_in[r, q].astype(jnp.float32)
@@ -341,11 +341,12 @@
             def _():
                 attend(r, reach, False)
 
-            project_out(r)
         if 0 <= r - 1 < CHUNKS:
             stage_one(r - 1)
         if 0 <= r - 2 < CHUNKS:
             stage_two(r - 2)
+        if r < CHUNKS:
+            project_out(r)
         if 0 <= r - 3 < CHUNKS:
             stage_three(r - 3)
 

time: 69.2 us -> 65.5 us (0.947)
  Pallas kernels: 67.2 us -> 63.4 us
    pallas_call x1, Pallas kernels: 67.2 us -> 63.4 us  [body(): pl.pallas_call(functools.partial(kernel, tok_size), out_shape=jax.ShapeDt...]
where the time goes in v3:
time: 65.5 us; the launch traced here: 65.3 us
  Pallas kernels  63.4 us (97%)
  local copies, waits for them, and re-layouts  1.87 us (3%)
    pallas_call x1, Pallas kernels, body(): pl.pallas_call(functools.partial(kernel, tok_size), out_shape=jax.ShapeDt...  63.4 us
    unnamed x1, local copies, waits for them, and re-layouts  1.87 us

profile of v3, /device:TPU:16, one launch (start us, length us, event | category | flops | bytes accessed | tf_op | source)
XLA Modules:
  0.0 65.3 jit_solution(9707415324277484704)
XLA Ops:
  0.0 63.4 %shard_map.73 = bf16[512,512]{1,0:T(8,128)(2,1)} custom-call(bf16[512,512]{1,0:T(8,128)(2,1)} %tokens_hbm.1, bf16[512]{0:T(512)(128)(2,1)} %gain_ref.1, bf16[8,512,768]{2,1,0:T(8,128)(2,1)} %bitcast.2, bf16[512,4096]{1,0:T(8,128)(2,1)} %wout_hbm.1, s32[1,512]{1,0:T(1,128)} %bitcast.3, f32[2,512,128]{2,1,0:T(8,128)} %constant.4.clone.local_ref, ...), custom_call_target="tpu_custom_call" | custom-call | tf_op jit(solution)/shard_map/pallas_call | solution.py:392
  63.4 1.9 %copy.9 = bf16[512,512]{1,0:T(8,128)(2,1)} copy(bf16[512,512]{1,0:T(8,128)(2,1)} %shard_map.73) | data formatting | bytes 1048576
